TPU v7x, 32 devices: a whole 2x2x4 slice. The times are simulated.
32 devices in a mesh: groups: 2 (over y), tile: 4 (over x, core), member: 4 (over z).
Axes of the slice: x: 2, y: 2, z: 4, core: 2. Of those that a mesh axis runs over, the one named last changes fastest.
Arguments:
- fields: bfloat16 [8, 6, 16, 16, 256], P(('groups', 'member'), None, 'tile'), parts along dimension 0, may hold values from -6 to 6
- weight: bfloat16 [2304, 256], P(('tile', 'member')), may hold values from -0.125 to 0.125
- cotangent: bfloat16 [8, 6, 16, 16, 256], P(('groups', 'member'), None, 'tile'), parts along dimension 0, may hold values from -6 to 6
- adjacency: int32 [6, 4, 3], replicated, may hold values from 0 to 5, as said below
Outputs:
- activation: bfloat16 [8, 6, 16, 16, 256], P(('groups', 'member'), None, 'tile'), parts along dimension 0
- input_grad: bfloat16 [8, 6, 16, 16, 256], P(('groups', 'member'), None, 'tile'), parts along dimension 0
- weight_grad: float32 [4608, 256], P(('groups', 'tile', 'member')), parts along dimension 0
There are 2 independent parts, one for each index of `groups`. A program takes and returns all parts, laid end to end along the dimension named above; an argument that names none is the same for every part. Nothing has to cross between parts.
Inputs may be any that keep to these rules, and one draw needn't show every extreme that they name: `adjacency`: each row names a face other than f, an edge 0 to 3 of it and a flag 0 or 1; the pairing is symmetric (edge e of f names edge k of g exactly when edge k of g names edge e of f, with the same flag) and sews the six faces into the surface of a cube.
All inputs are finite; a program needn't handle non-finite values.
Results may differ from a plain program's by a relative error of at most 0.005.
Values may be sent and summed in bfloat16 or wider, within the bound.
A program may use at most 128 MiB of HBM per device.

v0:
```python
import math
import jax
import jax.numpy as jnp
from jax import lax
from jax.sharding import PartitionSpec as P

gelu_scale = 0.7978845608028654


def from_root(value, axis, source):
    kept = jnp.where(lax.axis_index(axis) == source, value, 0).astype(value.dtype)
    return lax.psum(kept, axis)


def extended(cells, sides, width):
    for axis, dim in sides:
        count = lax.axis_size(axis)
        ends = count - 1
        head = lax.slice_in_dim(cells, 0, width, axis=dim)
        tail = lax.slice_in_dim(cells, cells.shape[dim] - width, cells.shape[dim], axis=dim)
        cells = jnp.concatenate(
            [
                lax.ppermute(tail, axis, [(i, (i + 1) % count) for i in range(ends)]),
                cells,
                lax.ppermute(head, axis, [((i + 1) % count, i) for i in range(ends)]),
            ],
            axis=dim,
        )
    return cells


def gelu_tanh(argument):
    return (
        0.5
        * argument
        * (1.0 + jnp.tanh(gelu_scale * (argument + 0.044715 * argument * argument * argument)))
    )


def edge_selector(adjacency):
    source_index = adjacency[:, :, 2] * 24 + adjacency[:, :, 0] * 4 + adjacency[:, :, 1]
    source_index = source_index.reshape(24)
    return (source_index[:, None] == jnp.arange(48, dtype=jnp.int32)[None, :]).astype(jnp.float32)


def route_lines(cycle_grad, selector):
    members, face_count, edges, face_size, channels = cycle_grad.shape
    flat_cycle = cycle_grad.reshape(members, 24, face_size, channels)
    routed = jnp.einsum("ts,mtfc->msfc", selector, flat_cycle, precision=lax.Precision.HIGHEST)
    line_grad = routed[:, :24] + routed[:, 24:, ::-1]
    return line_grad.reshape(members, face_count, 4, face_size, channels)


def shards(fields, weight, cotangent, adjacency):
    members, face_count, band_rows, face_size, channels = fields.shape
    position = lax.axis_index("tile")
    tile_count = lax.axis_size("tile")
    top_device = position == 0
    bottom_device = position == tile_count - 1
    row_start = position * band_rows
    selector = edge_selector(adjacency)
    full_weight = lax.all_gather(weight, ("tile", "member"), axis=0, tiled=True)
    side_columns = jnp.stack([fields[:, :, :, 0, :], fields[:, :, :, -1, :]], axis=2)
    all_columns = lax.all_gather(side_columns, "tile", axis=3, tiled=True)
    north_lines = from_root(fields[:, :, 0, :, :], "tile", 0)
    south_lines = from_root(fields[:, :, -1, :, :], "tile", tile_count - 1)
    edge_lines = jnp.concatenate(
        [north_lines[:, :, None], south_lines[:, :, None], all_columns], axis=2
    )
    edge_lines = edge_lines.reshape(members, 24, face_size, channels)
    both_ways = jnp.concatenate([edge_lines, edge_lines[:, :, ::-1]], axis=1)
    cycle_cells = jnp.einsum(
        "ts,msfc->mtfc",
        selector.astype(jnp.bfloat16),
        both_ways,
        preferred_element_type=jnp.float32,
    )
    cycle_cells = cycle_cells.astype(jnp.bfloat16).reshape(
        members, face_count, 4, face_size, channels
    )
    side_cycle = lax.dynamic_slice_in_dim(cycle_cells[:, :, 2:4], row_start, band_rows, 3)
    widened = jnp.concatenate(
        [side_cycle[:, :, 0][:, :, :, None], fields, side_cycle[:, :, 1][:, :, :, None]], axis=3
    )
    padded = extended(widened, (("tile", 2),), 1)
    zero_cell = jnp.zeros((members, face_count, 1, channels), jnp.bfloat16)
    north_row = jnp.concatenate([zero_cell, cycle_cells[:, :, 0], zero_cell], axis=2)
    south_row = jnp.concatenate([zero_cell, cycle_cells[:, :, 1], zero_cell], axis=2)
    padded = padded.at[:, :, 0].set(jnp.where(top_device, north_row, padded[:, :, 0]))
    padded = padded.at[:, :, -1].set(jnp.where(bottom_device, south_row, padded[:, :, -1]))
    cell_count = members * face_count * band_rows * face_size
    pre_act = jnp.zeros((cell_count, channels), jnp.float32)
    for row_step in range(3):
        for col_step in range(3):
            offset = 3 * row_step + col_step
            window = padded[
                :, :, row_step : row_step + band_rows, col_step : col_step + face_size
            ].reshape(cell_count, channels)
            pre_act = pre_act + jnp.dot(
                window,
                full_weight[offset * channels : (offset + 1) * channels],
                preferred_element_type=jnp.float32,
            )
    activation = gelu_tanh(pre_act).astype(jnp.bfloat16).reshape(fields.shape)
    unused_value, pullback = jax.vjp(gelu_tanh, pre_act)
    act_grad = pullback(cotangent.reshape(cell_count, channels).astype(jnp.float32))[0].astype(
        jnp.bfloat16
    )
    grad_terms = []
    grad_pad = jnp.zeros((members, face_count, band_rows + 2, face_size + 2, channels), jnp.float32)
    for row_step in range(3):
        for col_step in range(3):
            offset = 3 * row_step + col_step
            window = padded[
                :, :, row_step : row_step + band_rows, col_step : col_step + face_size
            ].reshape(cell_count, channels)
            grad_terms.append(
                lax.dot_general(
                    window, act_grad, (((0,), (0,)), ((), ())), preferred_element_type=jnp.float32
                )
            )
            kernel_rows = full_weight[offset * channels : (offset + 1) * channels]
            product_term = jnp.dot(act_grad, kernel_rows.T, preferred_element_type=jnp.float32)
            product_term = product_term.reshape(members, face_count, band_rows, face_size, channels)
            grad_pad = grad_pad.at[
                :, :, row_step : row_step + band_rows, col_step : col_step + face_size
            ].add(product_term)
    local_grad = jnp.concatenate(grad_terms, axis=0)
    owned_rows = lax.psum_scatter(local_grad, ("tile", "member"), scatter_dimension=0, tiled=True)
    total_cells = cell_count * tile_count * lax.axis_size("member")
    weight_grad = owned_rows / math.sqrt(total_cells)
    cycle_rows = jnp.stack([grad_pad[:, :, 0], grad_pad[:, :, -1]], axis=2)
    received = extended(cycle_rows, (("tile", 2),), 1)
    band_grad = grad_pad[:, :, 1:-1]
    band_grad = band_grad.at[:, :, 0].add(received[:, :, 0])
    band_grad = band_grad.at[:, :, -1].add(received[:, :, 3])
    side_grad = jnp.stack([band_grad[:, :, :, 0], band_grad[:, :, :, -1]], axis=2)
    side_full = lax.dynamic_update_slice_in_dim(
        jnp.zeros((members, face_count, 2, face_size, channels), jnp.float32),
        side_grad,
        row_start,
        3,
    )
    north_grad = jnp.where(top_device, grad_pad[:, :, 0, 1:-1], 0.0)
    south_grad = jnp.where(bottom_device, grad_pad[:, :, -1, 1:-1], 0.0)
    cycle_grad = jnp.concatenate(
        [north_grad[:, :, None], south_grad[:, :, None], side_full], axis=2
    )
    line_grad = route_lines(cycle_grad, selector)
    side_share = lax.psum_scatter(
        line_grad[:, :, 2:4].astype(jnp.bfloat16), "tile", scatter_dimension=3, tiled=True
    ).astype(jnp.float32)
    top_bottom = lax.psum(line_grad[:, :, 0:2].astype(jnp.bfloat16), "tile").astype(jnp.float32)
    cell_grad = band_grad[:, :, :, 1:-1]
    cell_grad = cell_grad.at[:, :, :, 0].add(side_share[:, :, 0])
    cell_grad = cell_grad.at[:, :, :, -1].add(side_share[:, :, 1])
    cell_grad = cell_grad.at[:, :, 0].add(jnp.where(top_device, top_bottom[:, :, 0], 0.0))
    cell_grad = cell_grad.at[:, :, -1].add(jnp.where(bottom_device, top_bottom[:, :, 1], 0.0))
    input_grad = cell_grad.astype(jnp.bfloat16)
    return (activation, input_grad, weight_grad)


def solution(mesh):
    in_specs = (
        P(("groups", "member"), None, "tile", None, None),
        P(("tile", "member"), None),
        P(("groups", "member"), None, "tile", None, None),
        P(),
    )
    out_specs = (
        P(("groups", "member"), None, "tile", None, None),
        P(("groups", "member"), None, "tile", None, None),
        P(("groups", "tile", "member"), None),
    )
    return jax.shard_map(shards, mesh=mesh, in_specs=in_specs, out_specs=out_specs, check_vma=False)
```

profile of v0, /device:TPU:0, one launch (start us, length us, event | category | flops | bytes accessed | tf_op | source)
XLA Modules:
  0.0 224.5 jit_solution(6184690400154656035)
XLA Ops:
  12.4 6.3 %all_gather.6 = bf16[1,6,2,16,256]{4,2,1,0,3:T(2,128)(2,1)S(1)} all-gather(bf16[1,6,2,4,256]{4,2,1,0,3:T(2,128)(2,1)S(1)} %copy.128), channel_id=1, replica_groups=mesh['groups'=2,'tile'=4,'member'=4] {'tile'}, dimensions={3}, use_global_device_ids=true | all-gather | bytes 122880 | tf_op jit(solution)/shard_map/all_gather | solution.py:64
  20.6 27.5 %all-reduce.7.cloned.1.call-done = (bf16[1,6,1,16,256]{4,2,1,3,0:T(2,128)(2,1)}, bf16[1,6,1,16,256]{4,2,1,3,0:T(2,128)(2,1)}) async-done(((bf16[1,6,1,16,256]{4,2,1,3,0:T(2,128)(2,1)}, bf16[1,6,1,16,256]{4,2,1,3,0:T(2,128)(2,1)}), (bf16[1,6,1,16,256]{4,2,1,3,0:T(2,128)(2,1)}, bf16[1,6,1,16,256]{4,2,1,3,0:T(2,128)(2,1)})) %all-reduce.7.cloned.1.call-update) | async-done | bytes 98320 | tf_op jit(solution)/shard_map/psum | solution.py:12
  51.6 3.0 %collective-permute-start = (bf16[1,6,1,18,256]{4,3,2,1,0:T(8,128)(2,1)S(1)}, bf16[1,6,1,18,256]{4,3,2,1,0:T(8,128)(2,1)S(1)}, u32[]{:S(2)}, u32[]{:S(2)}) collective-permute-start(bf16[1,6,1,18,256]{4,3,2,1,0:T(8,128)(2,1)S(1)} %get-tuple-element.240), channel_id=1, source_target_pairs={{0,4},{4,8},{8,12},{1,5},{5,9},{9,13},{2,6},{6,10},{10,14},{3,7},{... | collective-permute-start | bytes 165896 | tf_op jit(solution)/shard_map/ppermute | solution.py:23
  56.2 1.3 fusion.39
  62.6 1.4 copy_add_fusion
  64.1 6.5 %scatter-add.51 = f32[1,6,6,18,256]{4,2,1,3,0:T(8,128)S(1)} dynamic-update-slice(f32[1,6,6,18,256]{4,2,1,3,0:T(8,128)S(1)} %scatter-add.50, f32[1,6,4,16,256]{4,2,1,3,0:T(4,128)S(1)} %copy_add_fusion, s32[]{:T(128)} %constant.477.clone.1, s32[]{:T(128)} %constant.477.clone.1, s32[]{:T(128)} %bitcast.22, s32[]{:T(128)} %bitcast.23, s32[]{:T(128)} %constant.477.clone.1) | dynamic-update-slice | bytes 786436 | tf_op jit(solution)/shard_map/scatter-add | solution.py:127
  70.8 2.1 add_select_fusion
  72.9 6.4 %scatter-add.54 = f32[1,6,6,18,256]{4,2,1,3,0:T(8,128)S(1)} dynamic-update-slice(f32[1,6,6,18,256]{4,2,1,3,0:T(8,128)S(1)} %scatter-add.51, f32[1,6,4,16,256]{4,2,1,3,0:T(4,128)S(1)} %add_select_fusion, s32[]{:T(128)} %constant.477.clone.1, s32[]{:T(128)} %constant.477.clone.1, s32[]{:T(128)} %bitcast.25, s32[]{:T(128)} %bitcast.26, s32[]{:T(128)} %constant.477.clone.1) | dynamic-update-slice | bytes 786436 | tf_op jit(solution)/shard_map/scatter-add | solution.py:127
  80.8 5.5 %scatter-add.55 = f32[1,6,6,18,256]{4,2,1,3,0:T(8,128)S(1)} dynamic-update-slice(f32[1,6,6,18,256]{4,2,1,3,0:T(8,128)S(1)} %scatter-add.54, f32[1,6,4,16,256]{4,2,1,3,0:T(4,128)S(1)} %slice_add_fusion.6, s32[]{:T(128)} %constant.477.clone.1, s32[]{:T(128)} %constant.477.clone.1, s32[]{:T(128)} %constant.493.clone.1, s32[]{:T(128)} %constant.477.clone.1, s32[]{:T(128)} %constant.477.clone.1) | dynamic-update-slice | bytes 786436 | tf_op jit(solution)/shard_map/scatter-add | solution.py:127
  87.9 5.4 %scatter-add.56 = f32[1,6,6,18,256]{4,2,1,3,0:T(8,128)S(1)} dynamic-update-slice(f32[1,6,6,18,256]{4,2,1,3,0:T(8,128)S(1)} %scatter-add.55, f32[1,6,4,16,256]{4,2,1,3,0:T(4,128)S(1)} %slice_add_fusion.5, s32[]{:T(128)} %constant.477.clone.1, s32[]{:T(128)} %constant.477.clone.1, s32[]{:T(128)} %constant.493.clone.1, s32[]{:T(128)} %constant.493.clone.1, s32[]{:T(128)} %constant.477.clone.1) | dynamic-update-slice | bytes 786436 | tf_op jit(solution)/shard_map/scatter-add | solution.py:127
  94.7 5.2 %scatter-add.59 = f32[1,6,6,18,256]{4,2,1,3,0:T(8,128)S(1)} dynamic-update-slice(f32[1,6,6,18,256]{4,2,1,3,0:T(8,128)S(1)} %scatter-add.56, f32[1,6,4,16,256]{4,2,1,3,0:T(4,128)S(1)} %slice_add_fusion.4, s32[]{:T(128)} %constant.477.clone.1, s32[]{:T(128)} %constant.477.clone.1, s32[]{:T(128)} %constant.493.clone.1, s32[]{:T(128)} %constant.490.clone.1, s32[]{:T(128)} %constant.477.clone.1) | dynamic-update-slice | bytes 786436 | tf_op jit(solution)/shard_map/scatter-add | solution.py:127
  101.5 5.5 %scatter-add.60 = f32[1,6,6,18,256]{4,2,1,3,0:T(8,128)S(1)} dynamic-update-slice(f32[1,6,6,18,256]{4,2,1,3,0:T(8,128)S(1)} %scatter-add.59, f32[1,6,4,16,256]{4,2,1,3,0:T(4,128)S(1)} %slice_add_fusion.3, s32[]{:T(128)} %constant.477.clone.1, s32[]{:T(128)} %constant.477.clone.1, s32[]{:T(128)} %constant.490.clone.1, s32[]{:T(128)} %constant.477.clone.1, s32[]{:T(128)} %constant.477.clone.1) | dynamic-update-slice | bytes 786436 | tf_op jit(solution)/shard_map/scatter-add | solution.py:127
  108.5 5.4 %scatter-add.61 = f32[1,6,6,18,256]{4,2,1,3,0:T(8,128)S(1)} dynamic-update-slice(f32[1,6,6,18,256]{4,2,1,3,0:T(8,128)S(1)} %scatter-add.60, f32[1,6,4,16,256]{4,2,1,3,0:T(4,128)S(1)} %slice_add_fusion.2, s32[]{:T(128)} %constant.477.clone.1, s32[]{:T(128)} %constant.477.clone.1, s32[]{:T(128)} %constant.490.clone.1, s32[]{:T(128)} %constant.493.clone.1, s32[]{:T(128)} %constant.477.clone.1) | dynamic-update-slice | bytes 786436 | tf_op jit(solution)/shard_map/scatter-add | solution.py:127
  115.4 5.2 %scatter-add.64 = f32[1,6,6,18,256]{4,2,1,3,0:T(8,128)S(1)} dynamic-update-slice(f32[1,6,6,18,256]{4,2,1,3,0:T(8,128)S(1)} %scatter-add.61, f32[1,6,4,16,256]{4,2,1,3,0:T(4,128)S(1)} %slice_add_fusion.1, s32[]{:T(128)} %constant.477.clone.1, s32[]{:T(128)} %constant.477.clone.1, s32[]{:T(128)} %constant.490.clone.1, s32[]{:T(128)} %constant.490.clone.1, s32[]{:T(128)} %constant.477.clone.1) | dynamic-update-slice | bytes 786436 | tf_op jit(solution)/shard_map/scatter-add | solution.py:127
  123.5 2.8 %collective-permute-start.2 = (f32[1,6,1,18,256]{4,2,1,3,0:T(1,128)S(1)}, f32[1,6,1,18,256]{4,2,1,3,0:T(1,128)S(1)}, u32[]{:S(2)}, u32[]{:S(2)}) collective-permute-start(f32[1,6,1,18,256]{4,2,1,3,0:T(1,128)S(1)} %get-tuple-element.226), channel_id=1, source_target_pairs={{0,4},{4,8},{8,12},{1,5},{5,9},{9,13},{2,6},{6,10},{10,14},{3,7},{... | collective-permute-start | bytes 331784 | tf_op jit(solution)/shard_map/ppermute | solution.py:23
  126.3 1.6 collective-permute-start.3
  130.9 3.4 %scatter-add.65 = f32[1,6,4,18,256]{4,2,1,3,0:T(4,128)} dynamic-update-slice(f32[1,6,4,18,256]{4,2,1,3,0:T(4,128)} %slice.868, f32[1,6,1,18,256]{4,2,1,3,0:T(1,128)S(1)} %slice_add_fusion.8, s32[]{:T(128)} %constant.477.clone.1, s32[]{:T(128)} %constant.477.clone.1, s32[]{:T(128)} %constant.477.clone.1, s32[]{:T(128)} %constant.477.clone.1, s32[]{:T(128)} %constant.477.clone.1) | dynamic-update-slice | bytes 221188 | tf_op jit(solution)/shard_map/scatter-add | solution.py:135
  135.6 3.4 %scatter-add.66 = f32[1,6,4,18,256]{4,2,1,3,0:T(4,128)} dynamic-update-slice(f32[1,6,4,18,256]{4,2,1,3,0:T(4,128)} %scatter-add.65, f32[1,6,1,18,256]{4,2,1,3,0:T(1,128)S(1)} %slice_add_fusion.7, s32[]{:T(128)} %constant.477.clone.1, s32[]{:T(128)} %constant.477.clone.1, s32[]{:T(128)} %constant.479.clone.1, s32[]{:T(128)} %constant.477.clone.1, s32[]{:T(128)} %constant.477.clone.1) | dynamic-update-slice | bytes 221188 | tf_op jit(solution)/shard_map/scatter-add | solution.py:136
  143.8 1.4 copy-done.1
  146.6 33.7 %all-reduce.9.cloned.1.call-done = (bf16[1,6,2,16,256]{4,3,1,2,0:T(8,128)(2,1)}, bf16[1,6,2,16,256]{4,2,1,3,0:T(2,128)(2,1)}) async-done(((bf16[1,6,2,16,256]{4,3,1,2,0:T(8,128)(2,1)}, bf16[1,6,2,16,256]{4,2,1,3,0:T(2,128)(2,1)}), (bf16[1,6,2,16,256]{4,3,1,2,0:T(8,128)(2,1)}, bf16[1,6,2,16,256]{4,2,1,3,0:T(2,128)(2,1)})) %all-reduce.9.cloned.1.call-update) | async-done | bytes 196624
  182.3 2.8 %scatter-add.71 = f32[1,6,4,16,256]{4,2,1,3,0:T(4,128)S(1)} dynamic-update-slice(f32[1,6,4,16,256]{4,2,1,3,0:T(4,128)S(1)} %fusion.48, f32[1,6,1,16,256]{4,2,1,3,0:T(1,128)S(1)} %fusion.41, s32[]{:T(128)} %constant.477.clone.1, s32[]{:T(128)} %constant.477.clone.1, s32[]{:T(128)} %constant.477.clone.1, s32[]{:T(128)} %constant.477.clone.1, s32[]{:T(128)} %constant.477.clone.1) | dynamic-update-slice | bytes 196612 | tf_op jit(solution)/shard_map/scatter-add | solution.py:157
  185.3 2.8 %scatter-add.74 = f32[1,6,4,16,256]{4,2,1,3,0:T(4,128)S(1)} dynamic-update-slice(f32[1,6,4,16,256]{4,2,1,3,0:T(4,128)S(1)} %scatter-add.71, f32[1,6,1,16,256]{4,2,1,3,0:T(1,128)S(1)} %fusion.42, s32[]{:T(128)} %constant.477.clone.1, s32[]{:T(128)} %constant.477.clone.1, s32[]{:T(128)} %constant.479.clone.1, s32[]{:T(128)} %constant.477.clone.1, s32[]{:T(128)} %constant.477.clone.1) | dynamic-update-slice | bytes 196612 | tf_op jit(solution)/shard_map/scatter-add | solution.py:158
  188.9 26.6 %reduce-scatter.3.cloned.1.call-done = f32[144,256]{1,0:T(8,128)} async-done(((f32[2304,256]{1,0:T(8,128)}), f32[144,256]{1,0:T(8,128)}) %reduce-scatter.3.cloned.1.call-update) | async-done | bytes 147472 | tf_op jit(solution)/shard_map/reduce_scatter | solution.py:129
  215.5 1.6 broadcast_multiply_fusion
  (157 shorter events, 40.4 us)
Async XLA Ops:
  8.0 11.9 %copy-start.21 = (s32[5]{0:T(128)S(1)}, s32[5]{0:T(128)}, u32[]{:S(2)}) copy-start(s32[5]{0:T(128)} %constant.491.clone.1) | copy-start | bytes 64
  8.0 40.0 %all-reduce.7.cloned.1.call-start = ((), (), s32[]{:S(2)}) async-start(), calls=%async_computation.3 | async-start | bytes 393216 | tf_op jit(solution)/shard_map/psum | solution.py:12
  9.8 46.4 %all-gather.2.cloned.1.call-start = ((), (), s32[]{:S(2)}) async-start(), calls=%async_computation.1 | async-start | bytes 1253376 | tf_op jit(solution)/shard_map/all_gather | solution.py:62
  10.4 170.0 %all-reduce.9.cloned.1.call-start = ((), (), s32[]{:S(2)}) async-start(), calls=%async_computation.4 | async-start | bytes 393216
  50.3 4.5 %collective-permute-start.1 = (bf16[1,6,1,18,256]{4,3,2,1,0:T(8,128)(2,1)S(1)}, bf16[1,6,1,18,256]{4,3,2,1,0:T(8,128)(2,1)S(1)}, u32[]{:S(2)}, u32[]{:S(2)}) collective-permute-start(bf16[1,6,1,18,256]{4,3,2,1,0:T(8,128)(2,1)S(1)} %get-tuple-element.241), channel_id=1, source_target_pairs={{4,0},{8,4},{12,8},{5,1},{9,5},{13,9},{6,2},{10,6},{14,10},{7,3},{... | collective-permute-start | bytes 165896 | tf_op jit(solution)/shard_map/ppermute | solution.py:25
  51.6 3.9 %collective-permute-start = (bf16[1,6,1,18,256]{4,3,2,1,0:T(8,128)(2,1)S(1)}, bf16[1,6,1,18,256]{4,3,2,1,0:T(8,128)(2,1)S(1)}, u32[]{:S(2)}, u32[]{:S(2)}) collective-permute-start(bf16[1,6,1,18,256]{4,3,2,1,0:T(8,128)(2,1)S(1)} %get-tuple-element.240), channel_id=1, source_target_pairs={{0,4},{4,8},{8,12},{1,5},{5,9},{9,13},{2,6},{6,10},{10,14},{3,7},{... | collective-permute-start | bytes 165896 | tf_op jit(solution)/shard_map/ppermute | solution.py:23
  56.1 2.8 %copy-start.3 = (bf16[1,6,4,16,256]{4,3,2,1,0:T(8,128)(2,1)}, bf16[1,6,4,16,256]{4,3,2,1,0:T(8,128)(2,1)S(1)}, u32[]{:S(2)}) copy-start(bf16[1,6,4,16,256]{4,3,2,1,0:T(8,128)(2,1)S(1)} %get-tuple-element.237) | copy-start | bytes 589828
  56.1 2.8 %copy-start.14 = (bf16[1,6,4,16,256]{4,3,2,1,0:T(8,128)(2,1)}, bf16[1,6,4,16,256]{4,3,2,1,0:T(8,128)(2,1)S(1)}, u32[]{:S(2)}) copy-start(bf16[1,6,4,16,256]{4,3,2,1,0:T(8,128)(2,1)S(1)} %get-tuple-element.235) | copy-start | bytes 589828
  56.1 2.8 %copy-start.16 = (bf16[1,6,4,16,256]{4,3,2,1,0:T(8,128)(2,1)}, bf16[1,6,4,16,256]{4,3,2,1,0:T(8,128)(2,1)S(1)}, u32[]{:S(2)}) copy-start(bf16[1,6,4,16,256]{4,3,2,1,0:T(8,128)(2,1)S(1)} %get-tuple-element.236) | copy-start | bytes 589828
  56.1 2.8 %copy-start.12 = (bf16[1,6,4,16,256]{4,3,2,1,0:T(8,128)(2,1)}, bf16[1,6,4,16,256]{4,3,2,1,0:T(8,128)(2,1)S(1)}, u32[]{:S(2)}) copy-start(bf16[1,6,4,16,256]{4,3,2,1,0:T(8,128)(2,1)S(1)} %get-tuple-element.234) | copy-start | bytes 589828
  56.1 3.0 %copy-start.10 = (bf16[1,6,4,16,256]{4,3,2,1,0:T(8,128)(2,1)}, bf16[1,6,4,16,256]{4,3,2,1,0:T(8,128)(2,1)S(1)}, u32[]{:S(2)}) copy-start(bf16[1,6,4,16,256]{4,3,2,1,0:T(8,128)(2,1)S(1)} %get-tuple-element.233) | copy-start | bytes 589828
  56.2 3.3 %copy-start.8 = (bf16[1,6,4,16,256]{4,3,2,1,0:T(8,128)(2,1)}, bf16[1,6,4,16,256]{4,3,2,1,0:T(8,128)(2,1)S(1)}, u32[]{:S(2)}) copy-start(bf16[1,6,4,16,256]{4,3,2,1,0:T(8,128)(2,1)S(1)} %get-tuple-element.232) | copy-start | bytes 589828
  56.2 3.5 %copy-start.6 = (bf16[1,6,4,16,256]{4,3,2,1,0:T(8,128)(2,1)}, bf16[1,6,4,16,256]{4,3,2,1,0:T(8,128)(2,1)S(1)}, u32[]{:S(2)}) copy-start(bf16[1,6,4,16,256]{4,3,2,1,0:T(8,128)(2,1)S(1)} %get-tuple-element.231) | copy-start | bytes 589828
  56.2 3.7 %copy-start.4 = (bf16[1,6,4,16,256]{4,3,2,1,0:T(8,128)(2,1)}, bf16[1,6,4,16,256]{4,3,2,1,0:T(8,128)(2,1)S(1)}, u32[]{:S(2)}) copy-start(bf16[1,6,4,16,256]{4,3,2,1,0:T(8,128)(2,1)S(1)} %get-tuple-element.230) | copy-start | bytes 589828
  56.2 3.9 %copy-start.19 = (bf16[1,6,4,16,256]{4,3,2,1,0:T(8,128)(2,1)}, bf16[1,6,4,16,256]{4,3,2,1,0:T(8,128)(2,1)S(1)}, u32[]{:S(2)}) copy-start(bf16[1,6,4,16,256]{4,3,2,1,0:T(8,128)(2,1)S(1)} %get-tuple-element.229) | copy-start | bytes 589828
  120.6 7.3 %copy-start.17 = (bf16[1,6,4,16,256]{4,3,2,1,0:T(8,128)(2,1)S(1)}, bf16[1,6,4,16,256]{4,3,2,1,0:T(8,128)(2,1)}, u32[]{:S(2)}) copy-start(bf16[1,6,4,16,256]{4,3,2,1,0:T(8,128)(2,1)} %copy-done.16) | copy-start | bytes 589828
  120.6 7.6 %copy-start.15 = (bf16[1,6,4,16,256]{4,3,2,1,0:T(8,128)(2,1)S(1)}, bf16[1,6,4,16,256]{4,3,2,1,0:T(8,128)(2,1)}, u32[]{:S(2)}) copy-start(bf16[1,6,4,16,256]{4,3,2,1,0:T(8,128)(2,1)} %copy-done.14) | copy-start | bytes 589828
  121.4 7.0 %copy-start.13 = (bf16[1,6,4,16,256]{4,3,2,1,0:T(8,128)(2,1)S(1)}, bf16[1,6,4,16,256]{4,3,2,1,0:T(8,128)(2,1)}, u32[]{:S(2)}) copy-start(bf16[1,6,4,16,256]{4,3,2,1,0:T(8,128)(2,1)} %copy-done.12) | copy-start | bytes 589828
  122.3 6.5 %copy-start.11 = (bf16[1,6,4,16,256]{4,3,2,1,0:T(8,128)(2,1)S(1)}, bf16[1,6,4,16,256]{4,3,2,1,0:T(8,128)(2,1)}, u32[]{:S(2)}) copy-start(bf16[1,6,4,16,256]{4,3,2,1,0:T(8,128)(2,1)} %copy-done.10) | copy-start | bytes 589828
  123.5 7.2 %collective-permute-start.2 = (f32[1,6,1,18,256]{4,2,1,3,0:T(1,128)S(1)}, f32[1,6,1,18,256]{4,2,1,3,0:T(1,128)S(1)}, u32[]{:S(2)}, u32[]{:S(2)}) collective-permute-start(f32[1,6,1,18,256]{4,2,1,3,0:T(1,128)S(1)} %get-tuple-element.226), channel_id=1, source_target_pairs={{0,4},{4,8},{8,12},{1,5},{5,9},{9,13},{2,6},{6,10},{10,14},{3,7},{... | collective-permute-start | bytes 331784 | tf_op jit(solution)/shard_map/ppermute | solution.py:23
  126.3 2.8 %copy-start.9 = (bf16[1,6,4,16,256]{4,3,2,1,0:T(8,128)(2,1)S(1)}, bf16[1,6,4,16,256]{4,3,2,1,0:T(8,128)(2,1)}, u32[]{:S(2)}) copy-start(bf16[1,6,4,16,256]{4,3,2,1,0:T(8,128)(2,1)} %copy-done.8) | copy-start | bytes 589828
  126.3 8.0 %collective-permute-start.3 = (f32[1,6,1,18,256]{4,2,1,3,0:T(1,128)}, f32[1,6,1,18,256]{4,2,1,3,0:T(1,128)}, u32[]{:S(2)}, u32[]{:S(2)}) collective-permute-start(f32[1,6,1,18,256]{4,2,1,3,0:T(1,128)} %get-tuple-element.225), channel_id=1, source_target_pairs={{4,0},{8,4},{12,8},{5,1},{9,5},{13,9},{6,2},{10,6},{14,10},{7,3},{... | collective-permute-start | bytes 331784 | tf_op jit(solution)/shard_map/ppermute | solution.py:25
  143.4 72.0 %reduce-scatter.3.cloned.1.call-start = ((), (), s32[]{:S(2)}) async-start(), calls=%async_computation.2 | async-start | bytes 2506752 | tf_op jit(solution)/shard_map/reduce_scatter | solution.py:129
  143.8 2.8 %copy-start.2 = (f32[1,6,4,18,256]{4,2,1,3,0:T(4,128)S(1)}, f32[1,6,4,18,256]{4,2,1,3,0:T(4,128)}, u32[]{:S(2)}) copy-start(f32[1,6,4,18,256]{4,2,1,3,0:T(4,128)} %scatter-add.66) | copy-start | bytes 1327108
  (8 other events, 11.1 us)
Sparse Core Ops, SparseCore 0:
  11.8 36.2 all-reduce.6
  143.6 36.7 all-reduce.8
Sparse Core Ops, SparseCore 1:
  12.8 41.2 all-gather.1
  147.7 67.7 reduce-scatter.2
where the time goes:
time: 225 us; the launch traced here: 224 us
  waiting for transfers between devices  89 us (40%)
  local copies, waits for them, and re-layouts  69.7 us (31%)
  between operations  17.2 us (8%)
  other arithmetic  16.9 us (8%)
  matrix products  16.6 us (7%)
  starting transfers between devices  8.86 us (4%)
  blocking collectives  6.29 us (3%)
    scatter-add x9, local copies, waits for them, and re-layouts, shards(): grad_pad = grad_pad.at[:, :, row_step:row_step + band_rows, col_step:col_...  45.4 us
    unnamed x5, waiting for transfers between devices  34.3 us
    psum x1, waiting for transfers between devices, from_root(): return lax.psum(kept, axis)  27.5 us
    reduce_scatter x1, waiting for transfers between devices, shards(): lax.psum_scatter(local_grad, ('tile', 'member'), scatter_dimension=0, til...  26.6 us
    dot_general x9, matrix products, shards(): jnp.dot(act_grad, kernel_rows.T, preferred_element_type=jnp.float32)  7.52 us
    all_gather x1, blocking collectives, shards(): all_columns = lax.all_gather(side_columns, 'tile', axis=3, tiled=True)  6.29 us
    ppermute x2, starting transfers between devices, extended(): lax.ppermute(tail, axis, [(i, (i + 1) % count) for i in range(ends)])  5.79 us
    dot_general x9, matrix products, shards(): jnp.dot(window, full_weight[offset * channels:(offset + 1) * channels], p...  4.9 us
  transfers between devices with their start and end apart: 8, of which 4 were waited for; matrix products, arithmetic and copies ran while one was open for 10% of the time, Pallas kernels for 0%

commit v1 on v0

--- a/solution.py
+++ b/solution.py
@@ -61,7 +61,26 @@
     selector = edge_selector(adjacency)
     full_weight = lax.all_gather(weight, ("tile", "member"), axis=0, tiled=True)
     side_columns = jnp.stack([fields[:, :, :, 0, :], fields[:, :, :, -1, :]], axis=2)
-    all_columns = lax.all_gather(side_columns, "tile", axis=3, tiled=True)
+    size, mine, span = (lax.axis_size("tile"), lax.axis_index("tile"), side_columns.shape[3])
+    upward = [(i_2, (i_2 + 1) % size) for i_2 in range(size)]
+    behind = [(i_2, (i_2 - 1) % size) for i_2 in range(size)]
+    whole = jnp.zeros(
+        (*side_columns.shape[:3], size * span, *side_columns.shape[3 + 1 :]), side_columns.dtype
+    )
+    whole = lax.dynamic_update_slice_in_dim(whole, side_columns, mine * span, axis=3)
+    from_left = from_right = side_columns
+    middle = size // 2
+    for hop in range(1, middle + 1):
+        from_left = lax.ppermute(from_left, "tile", upward)
+        whole = lax.dynamic_update_slice_in_dim(
+            whole, from_left, (mine - hop) % size * span, axis=3
+        )
+        if hop < size - middle:
+            from_right = lax.ppermute(from_right, "tile", behind)
+            whole = lax.dynamic_update_slice_in_dim(
+                whole, from_right, (mine + hop) % size * span, axis=3
+            )
+    all_columns = whole
     north_lines = from_root(fields[:, :, 0, :, :], "tile", 0)
     south_lines = from_root(fields[:, :, -1, :, :], "tile", tile_count - 1)
     edge_lines = jnp.concatenate(

time: 225 us -> 223 us (level)
  waiting for transfers between devices: 89 us -> 154 us
  local copies, waits for them, and re-layouts: 69.7 us -> 16.4 us
  blocking collectives: 6.29 us -> 0 us
  matrix products: 16.6 us -> 11.2 us
  other arithmetic: 16.9 us -> 13.6 us
  starting transfers between devices: 8.86 us -> 11.8 us
    scatter-add x9 -> x1, local copies, waits for them, and re-layouts: 45.4 us -> 0.08 us  [shards(): grad_pad = grad_pad.at[:, :, row_step:row_step + band_rows, col_step:col_...]
    reduce_scatter x1, waiting for transfers between devices: 26.6 us -> 65.3 us  [shards(): lax.psum_scatter(local_grad, ('tile', 'member'), scatter_dimension=0, til...]
    unnamed x5, waiting for transfers between devices: 34.3 us -> 0.08 us
    psum x0 -> x1, waiting for transfers between devices: none -> 32 us  [shards(): lax.psum(line_grad[:, :, 0:2].astype(jnp.bfloat16), 'tile')]
    reduce_scatter x0 -> x1, waiting for transfers between devices: none -> 21.7 us  [shards(): lax.psum_scatter(line_grad[:, :, 2:4].astype(jnp.bfloat16), 'tile', scatt...]
    scatter-add x4 -> x0, local copies, waits for them, and re-layouts: 12.4 us -> none  [the longest x1 3.4 us: shards(): band_grad = band_grad.at[:, :, 0].add(received[:, :, 0])]
    all_gather x1 -> x0, blocking collectives: 6.29 us -> none  [shards(): all_columns = lax.all_gather(side_columns, 'tile', axis=3, tiled=True)]
    scatter-add x0 -> x12, other arithmetic: none -> 5.77 us  [the longest x8 5.62 us: shards(): grad_pad = grad_pad.at[:, :, row_step:row_step + band_rows, col_step:col_...]
  transfers between devices with their start and end apart: 8 -> 12, of which waited for: 4 -> 6; matrix products, arithmetic and copies ran while one was open for 10% -> 7% of each run, Pallas kernels for 0% -> 0%
where the time goes in v1:
time: 223 us
  waiting for transfers between devices  154 us (69%)
  local copies, waits for them, and re-layouts  16.4 us (7%)
  between operations  16.1 us (7%)
  other arithmetic  13.6 us (6%)
  starting transfers between devices  11.8 us (5%)
  matrix products  11.2 us (5%)
    reduce_scatter x1, waiting for transfers between devices, shards(): lax.psum_scatter(local_grad, ('tile', 'member'), scatter_dimension=0, til...  65.3 us
    psum x1, waiting for transfers between devices, shards(): lax.psum(line_grad[:, :, 0:2].astype(jnp.bfloat16), 'tile')  32 us
    psum x1, waiting for transfers between devices, from_root(): return lax.psum(kept, axis)  30.2 us
    reduce_scatter x1, waiting for transfers between devices, shards(): lax.psum_scatter(line_grad[:, :, 2:4].astype(jnp.bfloat16), 'tile', scatt...  21.7 us
    ppermute x2, starting transfers between devices, extended(): lax.ppermute(tail, axis, [(i, (i + 1) % count) for i in range(ends)])  5.9 us
    scatter-add x8, other arithmetic, shards(): grad_pad = grad_pad.at[:, :, row_step:row_step + band_rows, col_step:col_...  5.62 us
    unnamed x41, local copies, waits for them, and re-layouts  5.29 us
    dot_general x9, matrix products, shards(): jnp.dot(window, full_weight[offset * channels:(offset + 1) * channels], p...  4.93 us
  transfers between devices with their start and end apart: 12, of which 6 were waited for; matrix products, arithmetic and copies ran while one was open for 7% of the time, Pallas kernels for 0%

profile of v1, /device:TPU:0, one launch (start us, length us, event | category | flops | bytes accessed | tf_op | source)
XLA Modules:
  0.0 222.6 jit_solution(17710168339735408036)
XLA Ops:
  9.6 1.0 fusion.75
  11.2 2.0 collective-permute-start.1
  14.7 1.3 and_reduce_fusion
  17.5 30.2 %all-reduce.7.cloned.1.call-done = (bf16[1,6,1,16,256]{4,1,2,3,0:T(8,128)(2,1)}, bf16[1,6,1,16,256]{4,1,2,3,0:T(8,128)(2,1)}) async-done(((bf16[1,6,1,16,256]{4,1,2,3,0:T(8,128)(2,1)}, bf16[1,6,1,16,256]{4,1,2,3,0:T(8,128)(2,1)}), (bf16[1,6,1,16,256]{4,1,2,3,0:T(8,128)(2,1)}, bf16[1,6,1,16,256]{4,1,2,3,0:T(8,128)(2,1)})) %all-reduce.7.cloned.1.call-update) | async-done | bytes 98320 | tf_op jit(solution)/shard_map/psum | solution.py:12
  50.9 1.3 collective-permute-start.4
  52.2 3.0 %collective-permute-start.3 = (bf16[1,6,1,18,256]{4,3,2,1,0:T(8,128)(2,1)S(1)}, bf16[1,6,1,18,256]{4,3,2,1,0:T(8,128)(2,1)S(1)}, u32[]{:S(2)}, u32[]{:S(2)}) collective-permute-start(bf16[1,6,1,18,256]{4,3,2,1,0:T(8,128)(2,1)S(1)} %get-tuple-element.229), channel_id=1, source_target_pairs={{0,4},{4,8},{8,12},{1,5},{5,9},{9,13},{2,6},{6,10},{10,14},{3,7},{... | collective-permute-start | bytes 165896 | tf_op jit(solution)/shard_map/ppermute | solution.py:23
  56.8 1.4 fusion.53
  58.2 1.1 convolution_add_fusion.7
  61.1 1.2 fusion.13
  63.4 1.6 fusion.8
  65.2 2.0 fusion.1
  70.8 2.9 %collective-permute-start.5 = (f32[1,6,1,18,256]{4,1,2,3,0:T(8,128)S(1)}, f32[1,6,1,18,256]{4,1,2,3,0:T(8,128)S(1)}, u32[]{:S(2)}, u32[]{:S(2)}) collective-permute-start(f32[1,6,1,18,256]{4,1,2,3,0:T(8,128)S(1)} %get-tuple-element.215), channel_id=1, source_target_pairs={{0,4},{4,8},{8,12},{1,5},{5,9},{9,13},{2,6},{6,10},{10,14},{3,7},{... | collective-permute-start | bytes 331784 | tf_op jit(solution)/shard_map/ppermute | solution.py:23
  75.5 1.3 collective-permute-start.6
  77.0 3.6 %collective-permute-done.6 = f32[1,6,1,18,256]{4,1,2,3,0:T(8,128)S(1)} collective-permute-done((f32[1,6,1,18,256]{4,1,2,3,0:T(8,128)S(1)}, f32[1,6,1,18,256]{4,1,2,3,0:T(8,128)S(1)}, u32[]{:S(2)}, u32[]{:S(2)}) %collective-permute-start.6) | collective-permute-done | bytes 110624 | tf_op jit(solution)/shard_map/ppermute | solution.py:25
  82.0 1.6 convolution_bitcast_fusion
  84.3 1.7 reshape.960
  86.0 1.8 fusion.72
  88.8 1.6 copy.151
  90.8 1.4 copy-done.1
  92.3 32.0 %all-reduce.5.cloned.1.call-done = bf16[1,6,2,16,256]{4,1,2,3,0:T(8,128)(2,1)} async-done(((bf16[1,6,2,16,256]{4,1,2,3,0:T(8,128)(2,1)}), bf16[1,6,2,16,256]{4,1,2,3,0:T(8,128)(2,1)}) %all-reduce.5.cloned.1.call-update) | async-done | bytes 98320 | tf_op jit(solution)/shard_map/psum | solution.py:172
  124.2 0.9 convert_element_type.51
  125.2 21.7 %reduce-scatter.3.cloned.1.call-done = bf16[1,6,2,4,256]{4,1,2,0,3:T(8,128)(2,1)} async-done(((bf16[1,6,2,16,256]{4,1,2,0,3:T(8,128)(2,1)}), bf16[1,6,2,4,256]{4,1,2,0,3:T(8,128)(2,1)}) %reduce-scatter.3.cloned.1.call-update) | async-done | bytes 24592 | tf_op jit(solution)/shard_map/reduce_scatter | solution.py:169
  148.6 65.3 %reduce-scatter.5.cloned.1.call-done = f32[144,256]{1,0:T(8,128)} async-done(((f32[2304,256]{1,0:T(8,128)}), f32[144,256]{1,0:T(8,128)}) %reduce-scatter.5.cloned.1.call-update) | async-done | bytes 147472 | tf_op jit(solution)/shard_map/reduce_scatter | solution.py:148
  213.9 1.6 broadcast_multiply_fusion
  (145 shorter events, 23.2 us)
Async XLA Ops:
  8.0 39.7 %all-reduce.7.cloned.1.call-start = ((), (), s32[]{:S(2)}) async-start(), calls=%async_computation.6 | async-start | bytes 262144 | tf_op jit(solution)/shard_map/psum | solution.py:12
  9.6 47.2 %all-gather.2.cloned.1.call-start = ((), (), s32[]{:S(2)}) async-start(), calls=%async_computation.2 | async-start | bytes 1253376 | tf_op jit(solution)/shard_map/all_gather | solution.py:62
  10.7 6.1 %collective-permute-start = (bf16[1,6,2,4,256]{4,3,1,2,0:T(4,128)(2,1)S(1)}, bf16[1,6,2,4,256]{4,3,1,2,0:T(4,128)(2,1)S(1)}, u32[]{:S(2)}, u32[]{:S(2)}) collective-permute-start(bf16[1,6,2,4,256]{4,3,1,2,0:T(4,128)(2,1)S(1)} %pad_maximum_fusion.11), channel_id=1, source_target_pairs={{0,4},{4,8},{8,12},{12,0},{1,5},{5,9},{9,13},{13,1},{2,6},{6,10},{... | collective-permute-start | bytes 73736 | tf_op jit(solution)/shard_map/ppermute | solution.py:74
  11.2 6.3 %collective-permute-start.1 = (bf16[1,6,2,4,256]{4,3,1,2,0:T(4,128)(2,1)S(1)}, bf16[1,6,2,4,256]{4,3,1,2,0:T(4,128)(2,1)S(1)}, u32[]{:S(2)}, u32[]{:S(2)}) collective-permute-start(bf16[1,6,2,4,256]{4,3,1,2,0:T(4,128)(2,1)S(1)} %pad_maximum_fusion.11), channel_id=1, source_target_pairs={{0,12},{4,0},{8,4},{12,8},{1,13},{5,1},{9,5},{13,9},{2,14},{6,2},{... | collective-permute-start | bytes 73736 | tf_op jit(solution)/shard_map/ppermute | solution.py:79
  13.2 111.0 %all-reduce.5.cloned.1.call-start = ((), (), s32[]{:S(2)}) async-start(), calls=%async_computation.4 | async-start | bytes 262144 | tf_op jit(solution)/shard_map/psum | solution.py:172
  16.8 32.7 %collective-permute-start.2 = (bf16[1,6,2,4,256]{4,3,1,2,0:T(4,128)(2,1)S(1)}, bf16[1,6,2,4,256]{4,3,1,2,0:T(4,128)(2,1)S(1)}, u32[]{:S(2)}, u32[]{:S(2)}) collective-permute-start(bf16[1,6,2,4,256]{4,3,1,2,0:T(4,128)(2,1)S(1)} %collective-permute-done), channel_id=1, source_target_pairs={{0,4},{4,8},{8,12},{12,0},{1,5},{5,9},{9,13},{13,1},{2,6},{6,10},{... | collective-permute-start | bytes 73736 | tf_op jit(solution)/shard_map/ppermute | solution.py:74
  50.9 4.5 %collective-permute-start.4 = (bf16[1,6,1,18,256]{4,3,2,1,0:T(8,128)(2,1)S(1)}, bf16[1,6,1,18,256]{4,3,2,1,0:T(8,128)(2,1)S(1)}, u32[]{:S(2)}, u32[]{:S(2)}) collective-permute-start(bf16[1,6,1,18,256]{4,3,2,1,0:T(8,128)(2,1)S(1)} %get-tuple-element.230), channel_id=1, source_target_pairs={{4,0},{8,4},{12,8},{5,1},{9,5},{13,9},{6,2},{10,6},{14,10},{7,3},{... | collective-permute-start | bytes 165896 | tf_op jit(solution)/shard_map/ppermute | solution.py:25
  52.2 3.9 %collective-permute-start.3 = (bf16[1,6,1,18,256]{4,3,2,1,0:T(8,128)(2,1)S(1)}, bf16[1,6,1,18,256]{4,3,2,1,0:T(8,128)(2,1)S(1)}, u32[]{:S(2)}, u32[]{:S(2)}) collective-permute-start(bf16[1,6,1,18,256]{4,3,2,1,0:T(8,128)(2,1)S(1)} %get-tuple-element.229), channel_id=1, source_target_pairs={{0,4},{4,8},{8,12},{1,5},{5,9},{9,13},{2,6},{6,10},{10,14},{3,7},{... | collective-permute-start | bytes 165896 | tf_op jit(solution)/shard_map/ppermute | solution.py:23
  56.7 2.8 %copy-start.8 = (bf16[1,6,4,16,256]{4,3,2,1,0:T(8,128)(2,1)}, bf16[1,6,4,16,256]{4,3,2,1,0:T(8,128)(2,1)S(1)}, u32[]{:S(2)}) copy-start(bf16[1,6,4,16,256]{4,3,2,1,0:T(8,128)(2,1)S(1)} %get-tuple-element.224) | copy-start | bytes 589828
  56.7 2.8 %copy-start.10 = (bf16[1,6,4,16,256]{4,3,2,1,0:T(8,128)(2,1)}, bf16[1,6,4,16,256]{4,3,2,1,0:T(8,128)(2,1)S(1)}, u32[]{:S(2)}) copy-start(bf16[1,6,4,16,256]{4,3,2,1,0:T(8,128)(2,1)S(1)} %get-tuple-element.225) | copy-start | bytes 589828
  56.7 2.8 %copy-start.6 = (bf16[1,6,4,16,256]{4,3,2,1,0:T(8,128)(2,1)}, bf16[1,6,4,16,256]{4,3,2,1,0:T(8,128)(2,1)S(1)}, u32[]{:S(2)}) copy-start(bf16[1,6,4,16,256]{4,3,2,1,0:T(8,128)(2,1)S(1)} %get-tuple-element.223) | copy-start | bytes 589828
  56.7 3.0 %copy-start.4 = (bf16[1,6,4,16,256]{4,3,2,1,0:T(8,128)(2,1)}, bf16[1,6,4,16,256]{4,3,2,1,0:T(8,128)(2,1)S(1)}, u32[]{:S(2)}) copy-start(bf16[1,6,4,16,256]{4,3,2,1,0:T(8,128)(2,1)S(1)} %get-tuple-element.222) | copy-start | bytes 589828
  56.7 3.7 %copy-start.2 = (bf16[1,6,4,16,256]{4,3,2,1,0:T(8,128)(2,1)}, bf16[1,6,4,16,256]{4,3,2,1,0:T(8,128)(2,1)S(1)}, u32[]{:S(2)}) copy-start(bf16[1,6,4,16,256]{4,3,2,1,0:T(8,128)(2,1)S(1)} %get-tuple-element.219) | copy-start | bytes 589828
  56.8 3.9 %copy-start.13 = (bf16[1,6,4,16,256]{4,3,2,1,0:T(8,128)(2,1)}, bf16[1,6,4,16,256]{4,3,2,1,0:T(8,128)(2,1)S(1)}, u32[]{:S(2)}) copy-start(bf16[1,6,4,16,256]{4,3,2,1,0:T(8,128)(2,1)S(1)} %get-tuple-element.218) | copy-start | bytes 589828
  70.4 3.3 %copy-start.11 = (bf16[1,6,4,16,256]{4,3,2,1,0:T(8,128)(2,1)S(1)}, bf16[1,6,4,16,256]{4,3,2,1,0:T(8,128)(2,1)}, u32[]{:S(2)}) copy-start(bf16[1,6,4,16,256]{4,3,2,1,0:T(8,128)(2,1)} %copy-done.10) | copy-start | bytes 589828
  70.4 3.6 %copy-start.9 = (bf16[1,6,4,16,256]{4,3,2,1,0:T(8,128)(2,1)S(1)}, bf16[1,6,4,16,256]{4,3,2,1,0:T(8,128)(2,1)}, u32[]{:S(2)}) copy-start(bf16[1,6,4,16,256]{4,3,2,1,0:T(8,128)(2,1)} %copy-done.8) | copy-start | bytes 589828
  70.8 3.5 %copy-start.7 = (bf16[1,6,4,16,256]{4,3,2,1,0:T(8,128)(2,1)S(1)}, bf16[1,6,4,16,256]{4,3,2,1,0:T(8,128)(2,1)}, u32[]{:S(2)}) copy-start(bf16[1,6,4,16,256]{4,3,2,1,0:T(8,128)(2,1)} %copy-done.6) | copy-start | bytes 589828
  70.8 3.7 %copy-start.5 = (bf16[1,6,4,16,256]{4,3,2,1,0:T(8,128)(2,1)S(1)}, bf16[1,6,4,16,256]{4,3,2,1,0:T(8,128)(2,1)}, u32[]{:S(2)}) copy-start(bf16[1,6,4,16,256]{4,3,2,1,0:T(8,128)(2,1)} %copy-done.4) | copy-start | bytes 589828
  70.8 6.1 %collective-permute-start.5 = (f32[1,6,1,18,256]{4,1,2,3,0:T(8,128)S(1)}, f32[1,6,1,18,256]{4,1,2,3,0:T(8,128)S(1)}, u32[]{:S(2)}, u32[]{:S(2)}) collective-permute-start(f32[1,6,1,18,256]{4,1,2,3,0:T(8,128)S(1)} %get-tuple-element.215), channel_id=1, source_target_pairs={{0,4},{4,8},{8,12},{1,5},{5,9},{9,13},{2,6},{6,10},{10,14},{3,7},{... | collective-permute-start | bytes 331784 | tf_op jit(solution)/shard_map/ppermute | solution.py:23
  75.5 5.1 %collective-permute-start.6 = (f32[1,6,1,18,256]{4,1,2,3,0:T(8,128)S(1)}, f32[1,6,1,18,256]{4,1,2,3,0:T(8,128)S(1)}, u32[]{:S(2)}, u32[]{:S(2)}) collective-permute-start(f32[1,6,1,18,256]{4,1,2,3,0:T(8,128)S(1)} %get-tuple-element.214), channel_id=1, source_target_pairs={{4,0},{8,4},{12,8},{5,1},{9,5},{13,9},{6,2},{10,6},{14,10},{7,3},{... | collective-permute-start | bytes 331784 | tf_op jit(solution)/shard_map/ppermute | solution.py:25
  83.6 5.0 %copy-start.3 = (bf16[1,6,4,16,256]{4,3,2,1,0:T(8,128)(2,1)S(1)}, bf16[1,6,4,16,256]{4,3,2,1,0:T(8,128)(2,1)}, u32[]{:S(2)}) copy-start(bf16[1,6,4,16,256]{4,3,2,1,0:T(8,128)(2,1)} %copy-done.2) | copy-start | bytes 589828
  84.3 6.2 %copy-start.14 = (bf16[1,6,4,16,256]{4,3,2,1,0:T(8,128)(2,1)S(1)}, bf16[1,6,4,16,256]{4,3,2,1,0:T(8,128)(2,1)}, u32[]{:S(2)}) copy-start(bf16[1,6,4,16,256]{4,3,2,1,0:T(8,128)(2,1)} %copy-done.13) | copy-start | bytes 589828
  88.5 58.3 %reduce-scatter.3.cloned.1.call-start = ((), (), s32[]{:S(2)}) async-start(), calls=%async_computation.3 | async-start | bytes 163840 | tf_op jit(solution)/shard_map/reduce_scatter | solution.py:169
  90.4 123.5 %reduce-scatter.5.cloned.1.call-start = ((), (), s32[]{:S(2)}) async-start(), calls=%async_computation.5 | async-start | bytes 2506752 | tf_op jit(solution)/shard_map/reduce_scatter | solution.py:148
  (4 other events, 5.8 us)
Sparse Core Ops, SparseCore 0:
  11.8 35.8 all-reduce.6
  88.6 35.5 all-reduce.4
  127.2 19.5 reduce-scatter.2
  150.9 62.9 reduce-scatter.4
Sparse Core Ops, SparseCore 1:
  13.3 40.5 all-gather.1
